TPU v7x, 32 devices: a whole 2x2x4 slice. The times are simulated.
32 devices in a mesh: seq: 8 (over y, x, core), row: 4 (over z).
Axes of the slice: x: 2, y: 2, z: 4, core: 2. Of those that a mesh axis runs over, the one named last changes fastest.
Arguments:
- block_input: bfloat16 [16, 1024, 512], P('row', 'seq'), may hold values from -6 to 6
- segment_ids: int32 [16, 1024], P('row'), may hold values from 0 to 1, as said below
- ln1_gain: float32 [512], replicated, may hold values from 0.5 to 1.5
- ln1_shift: float32 [512], replicated, may hold values from -1.5 to 1.5
- w_qkv: bfloat16 [512, 1536], replicated, may hold values from -0.375 to 0.375
- bias_query: float32 [512], replicated, may hold values from -1.5 to 1.5
- bias_value: float32 [512], replicated, may hold values from -1.5 to 1.5
- w_out: bfloat16 [512, 512], replicated, may hold values from -1 to 1
- bias_out: float32 [512], replicated, may hold values from -1.5 to 1.5
- ln2_gain: float32 [512], replicated, may hold values from 0.5 to 1.5
- ln2_shift: float32 [512], replicated, may hold values from -1.5 to 1.5
- w_up: bfloat16 [512, 2048], replicated, may hold values from -0.25 to 0.25
- bias_up: float32 [2048], replicated, may hold values from -1.5 to 1.5
- w_down: bfloat16 [2048, 512], replicated, may hold values from -0.125 to 0.125
- bias_down: float32 [512], replicated, may hold values from -1.5 to 1.5
- out_grad: bfloat16 [16, 1024, 512], P('row', 'seq'), may hold values from -6 to 6
Outputs:
- output: bfloat16 [16, 1024, 512], P('row', 'seq')
- input_grad: bfloat16 [16, 1024, 512], P('row', 'seq')
- grad_ln1_gain: float32 [512], replicated
- grad_ln1_shift: float32 [512], replicated
- grad_w_qkv: float32 [512, 1536], replicated
- grad_bias_query: float32 [512], replicated
- grad_bias_value: float32 [512], replicated
- grad_w_out: float32 [512, 512], replicated
- grad_bias_out: float32 [512], replicated
- grad_ln2_gain: float32 [512], replicated
- grad_ln2_shift: float32 [512], replicated
- grad_w_up: float32 [512, 2048], replicated
- grad_bias_up: float32 [2048], replicated
- grad_w_down: float32 [2048, 512], replicated
- grad_bias_down: float32 [512], replicated
Inputs may be any that keep to these rules, and one draw needn't show every extreme that they name: `segment_ids`: ids start at 0 and never fall along a row, rising by one at each new crop; equal ids mark one crop, whose tokens attend only to each other; in each aligned group of 4 rows one row, drawn from the seed, is a single crop, and every other row holds exactly 1024 // (4 * 128) crops.
All inputs are finite; a program needn't handle non-finite values.
Results may differ from a plain program's by a relative error of at most 0.015.
Values may be sent and summed in bfloat16 or wider, within the bound.
No kernel may reach another device: no remote copies, remote signals or barrier semaphores. Data moves between devices by JAX's collectives and lax.ppermute only.
A program may use at most 256 MiB of HBM per device.

v0:
```python
import jax
import jax.numpy as jnp
from jax import lax
from jax.sharding import PartitionSpec as P

HEADS = 8


EPSILON = 1e-06
NEGATIVE = -1e30


def layer_norm(inputs, scaling, offset_row):
    centre = jnp.mean(inputs, axis=-1, keepdims=True)
    centred = inputs - centre
    spread = jnp.mean(centred * centred, axis=-1, keepdims=True)
    return centred * lax.rsqrt(spread + EPSILON) * scaling + offset_row


def smooth_gelu(inputs):
    return jax.nn.gelu(inputs, approximate=True)


def outer_sum(left_side, right_side):
    return lax.dot_general(
        left_side, right_side, (((0,), (0,)), ((), ())), preferred_element_type=jnp.float32
    )


def times_transposed(left_side, right_side):
    return lax.dot_general(
        left_side, right_side, (((1,), (1,)), ((), ())), preferred_element_type=jnp.float32
    )


def heads_last(stat_value):
    return jnp.transpose(stat_value, (0, 2, 1, 3))


def per_device(
    block_input,
    segment_ids,
    ln1_gain,
    ln1_shift,
    w_qkv,
    bias_query,
    bias_value,
    w_out,
    bias_out,
    ln2_gain,
    ln2_shift,
    w_up,
    bias_up,
    w_down,
    bias_down,
    out_grad,
):
    row_count, band_size, model_width = block_input.shape
    seq_length = segment_ids.shape[1]
    head_count = HEADS
    head_size = model_width // head_count
    score_scale = head_size ** (-0.5)
    token_count = row_count * band_size
    key_block = min(512, seq_length)
    block_count = seq_length // key_block
    band_start = lax.axis_index("seq") * band_size
    own_segments = lax.dynamic_slice_in_dim(segment_ids, band_start, band_size, 1)
    stat_shape = (row_count, head_count, band_size, 1)
    head_shape = (row_count, band_size, head_count, head_size)
    inputs = block_input.astype(jnp.float32).reshape(token_count, model_width)
    normed, norm_one_pull = jax.vjp(layer_norm, inputs, ln1_gain, ln1_shift)
    normed_low = normed.astype(jnp.bfloat16)
    packed = jnp.dot(normed_low, w_qkv, preferred_element_type=jnp.float32)
    queries = ((packed[:, :model_width] + bias_query) * score_scale).astype(jnp.bfloat16)
    keys_band = (
        packed[:, model_width : 2 * model_width]
        .astype(jnp.bfloat16)
        .reshape(row_count, band_size, model_width)
    )
    values_band = (
        (packed[:, 2 * model_width :] + bias_value)
        .astype(jnp.bfloat16)
        .reshape(row_count, band_size, model_width)
    )
    all_keys, all_values = (
        lax.all_gather(keys_band, "seq", axis=1, tiled=True),
        lax.all_gather(values_band, "seq", axis=1, tiled=True),
    )
    query_heads = queries.reshape(head_shape)

    def key_slices(block_index):
        offset = block_index * key_block
        key_part = lax.dynamic_slice_in_dim(all_keys, offset, key_block, 1).reshape(
            row_count, key_block, head_count, head_size
        )
        value_part = lax.dynamic_slice_in_dim(all_values, offset, key_block, 1).reshape(
            row_count, key_block, head_count, head_size
        )
        segment_part = lax.dynamic_slice_in_dim(segment_ids, offset, key_block, 1)
        allowed = own_segments[:, None, :, None] == segment_part[:, None, None, :]
        scores = jnp.einsum(
            "rbhd,rkhd->rhbk", query_heads, key_part, preferred_element_type=jnp.float32
        )
        return (jnp.where(allowed, scores, NEGATIVE), key_part, value_part)

    def running(state_triple, block_index):
        biggest, denominator, accumulated = state_triple
        scores, key_part, value_part = key_slices(block_index)
        newest = jnp.maximum(biggest, jnp.max(scores, axis=-1, keepdims=True))
        rescale = jnp.exp(biggest - newest)
        exponents = jnp.exp(scores - newest)
        denominator = denominator * rescale + jnp.sum(exponents, axis=-1, keepdims=True)
        accumulated = accumulated * heads_last(rescale) + jnp.einsum(
            "rhbk,rkhd->rbhd",
            exponents.astype(jnp.bfloat16),
            value_part,
            preferred_element_type=jnp.float32,
        )
        return ((newest, denominator, accumulated), None)

    blocks = jnp.arange(block_count)
    start_state = (
        jnp.full(stat_shape, NEGATIVE, jnp.float32),
        jnp.zeros(stat_shape, jnp.float32),
        jnp.zeros(head_shape, jnp.float32),
    )
    (biggest, denominator, accumulated), _ = lax.scan(running, start_state, blocks)

    def probabilities_of(scores):
        return jnp.exp(scores - biggest) / denominator

    attention_mix = accumulated / heads_last(denominator)
    mix_low = attention_mix.astype(jnp.bfloat16).reshape(token_count, model_width)
    attended = jnp.dot(mix_low, w_out, preferred_element_type=jnp.float32) + bias_out
    middle = inputs + attended
    normed_two, norm_two_pull = jax.vjp(layer_norm, middle, ln2_gain, ln2_shift)
    normed_two_low = normed_two.astype(jnp.bfloat16)
    hidden = jnp.dot(normed_two_low, w_up, preferred_element_type=jnp.float32) + bias_up
    active, gelu_pull = jax.vjp(smooth_gelu, hidden)
    active_low = active.astype(jnp.bfloat16)
    output = middle + jnp.dot(active_low, w_down, preferred_element_type=jnp.float32) + bias_down
    result = output.astype(jnp.bfloat16).reshape(row_count, band_size, model_width)
    grad_low = out_grad.reshape(token_count, model_width)
    grad_out = grad_low.astype(jnp.float32)
    grad_down = outer_sum(active_low, grad_low)
    grad_bias_down = jnp.sum(grad_out, axis=0)
    grad_active = times_transposed(grad_low, w_down)
    grad_hidden = gelu_pull(grad_active)[0].astype(jnp.bfloat16)
    grad_up = outer_sum(normed_two_low, grad_hidden)
    grad_bias_up = jnp.sum(grad_hidden.astype(jnp.float32), axis=0)
    grad_normed_two = times_transposed(grad_hidden, w_up)
    grad_middle, grad_ln2_gain, grad_ln2_shift = norm_two_pull(grad_normed_two)
    grad_middle = grad_middle + grad_out
    grad_attended = grad_middle.astype(jnp.bfloat16)
    grad_w_out = outer_sum(mix_low, grad_attended)
    grad_bias_out = jnp.sum(grad_attended.astype(jnp.float32), axis=0)
    grad_mix_flat = times_transposed(grad_attended, w_out).astype(jnp.bfloat16)
    grad_mix = grad_mix_flat.reshape(head_shape)
    inner_sum = heads_last(
        jnp.sum(grad_mix.astype(jnp.float32) * attention_mix, axis=-1, keepdims=True)
    )

    def local_grads(state_triple, block_index):
        grad_query, key_buffer, value_buffer = state_triple
        scores, key_part, value_part = key_slices(block_index)
        probabilities = probabilities_of(scores)
        slopes = jnp.einsum(
            "rbhd,rkhd->rhbk", grad_mix, value_part, preferred_element_type=jnp.float32
        )
        grad_scores = (probabilities * (slopes - inner_sum)).astype(jnp.bfloat16)
        grad_query = grad_query + jnp.einsum(
            "rhbk,rkhd->rbhd", grad_scores, key_part, preferred_element_type=jnp.float32
        )
        grad_key = jnp.einsum(
            "rhbk,rbhd->rkhd", grad_scores, query_heads, preferred_element_type=jnp.float32
        )
        grad_value = jnp.einsum(
            "rhbk,rbhd->rkhd",
            probabilities.astype(jnp.bfloat16),
            grad_mix,
            preferred_element_type=jnp.float32,
        )
        offset = block_index * key_block
        key_buffer = lax.dynamic_update_slice_in_dim(
            key_buffer, grad_key.reshape(row_count, key_block, model_width), offset, 1
        )
        value_buffer = lax.dynamic_update_slice_in_dim(
            value_buffer, grad_value.reshape(row_count, key_block, model_width), offset, 1
        )
        return ((grad_query, key_buffer, value_buffer), None)

    empty_row = jnp.zeros((row_count, seq_length, model_width), jnp.float32)
    (grad_query, key_terms, value_terms), _ = lax.scan(
        local_grads, (jnp.zeros(head_shape, jnp.float32), empty_row, empty_row), blocks
    )
    grad_key_band, grad_value_band = (
        lax.psum_scatter(
            key_terms.astype(jnp.bfloat16), "seq", scatter_dimension=1, tiled=True
        ).astype(jnp.float32),
        lax.psum_scatter(
            value_terms.astype(jnp.bfloat16), "seq", scatter_dimension=1, tiled=True
        ).astype(jnp.float32),
    )
    grad_query_low = grad_query.astype(jnp.bfloat16).reshape(token_count, model_width) * score_scale
    grad_key_low = grad_key_band.astype(jnp.bfloat16).reshape(token_count, model_width)
    grad_value_low = grad_value_band.astype(jnp.bfloat16).reshape(token_count, model_width)
    grad_packed = jnp.concatenate([grad_query_low, grad_key_low, grad_value_low], axis=1)
    grad_w_qkv = outer_sum(normed_low, grad_packed)
    grad_bias_query = jnp.sum(grad_query_low.astype(jnp.float32), axis=0)
    grad_bias_value = jnp.sum(grad_value_low.astype(jnp.float32), axis=0)
    grad_normed = times_transposed(grad_packed, w_qkv)
    grad_inputs, grad_ln1_gain, grad_ln1_shift = norm_one_pull(grad_normed)
    input_grad = (
        (grad_middle + grad_inputs).astype(jnp.bfloat16).reshape(row_count, band_size, model_width)
    )
    summed = lax.psum(
        (
            grad_ln1_gain,
            grad_ln1_shift,
            grad_w_qkv,
            grad_bias_query,
            grad_bias_value,
            grad_w_out,
            grad_bias_out,
            grad_ln2_gain,
            grad_ln2_shift,
            grad_up,
            grad_bias_up,
            grad_down,
            grad_bias_down,
        ),
        ("seq", "row"),
    )
    return (
        result,
        input_grad,
        summed[0],
        summed[1],
        summed[2],
        summed[3],
        summed[4],
        summed[5],
        summed[6],
        summed[7],
        summed[8],
        summed[9],
        summed[10],
        summed[11],
        summed[12],
    )


def solution(mesh):
    placed = (
        P("row", "seq", None),
        P("row", None),
        P(),
        P(),
        P(),
        P(),
        P(),
        P(),
        P(),
        P(),
        P(),
        P(),
        P(),
        P(),
        P(),
        P("row", "seq", None),
    )
    return jax.shard_map(
        per_device,
        mesh=mesh,
        in_specs=placed,
        out_specs=(
            P("row", "seq", None),
            P("row", "seq", None),
            P(),
            P(),
            P(),
            P(),
            P(),
            P(),
            P(),
            P(),
            P(),
            P(),
            P(),
            P(),
            P(),
        ),
        check_vma=False,
    )
```

profile of v0, /device:TPU:0, one launch (start us, length us, event | category | flops | bytes accessed | tf_op | source)
XLA Modules:
  0.0 605.4 jit_solution(1323431538982598880)
XLA Ops:
  24.3 33.8 %all-gather.3.cloned.1.call-done = bf16[4,1024,512]{1,2,0:T(8,128)(2,1)} async-done(((bf16[4,128,512]{1,2,0:T(8,128)(2,1)}), bf16[4,1024,512]{1,2,0:T(8,128)(2,1)}) %all-gather.3.cloned.1.call-update) | async-done | bytes 4194320 | tf_op jit(solution)/shard_map/all_gather | solution.py:86
  58.1 39.9 %all-gather.5.cloned.1.call-done = bf16[4,1024,512]{1,2,0:T(8,128)(2,1)} async-done(((bf16[4,128,512]{1,2,0:T(8,128)(2,1)}), bf16[4,1024,512]{1,2,0:T(8,128)(2,1)}) %all-gather.5.cloned.1.call-update) | async-done | bytes 4194320 | tf_op jit(solution)/shard_map/all_gather | solution.py:87
  98.0 42.4 %while.30 = (s32[]{:T(128)}, f32[4,8,128,1]{2,1,0,3:T(8,128)S(1)}, f32[4,8,128,1]{2,1,0,3:T(8,128)S(1)}, f32[4,128,8,64]{1,3,2,0:T(8,128)}, s32[4,128]{1,0:T(4,1...) while((s32[]{:T(128)}, f32[4,8,128,1]{2,1,0,3:T(8,128)S(1)}, ...), condition=%wide.region_5.6_spmd.clone, body=%wide.region_2.5_spmd.clone.sunk | while | flops 554721280 | bytes 75262200 | solution.py:127
  99.6 3.8 constant_dynamic-slice_fusion.13
  103.4 5.0 fusion.115
  108.4 5.1 fusion.117
  114.2 4.9 fusion.118
  124.5 5.0 fusion.115
  129.5 5.1 fusion.117
  135.2 5.2 fusion.118
  146.0 4.4 convert_reduce_fusion
  167.3 73.5 %while.31 = (s32[]{:T(128)}, f32[4,128,8,64]{1,3,2,0:T(8,128)}, bf16[4,1024,512]{2,1,0:T(8,128)(2,1)}, bf16[4,1024,512]{2,1,0:T(8,128)(2,1)}, s32[2]{0:T(128)S(1...) while((s32[]{:T(128)}, f32[4,128,8,64]{1,3,2,0:T(8,128)}, ...), condition=%wide.region_12.13_spmd.clone, body=%wide.region_11.12_spmd.clone.sunk | while | flops 1357643776 | bytes 170469760 | solution.py:193
  173.5 4.1 fusion.130
  177.6 4.9 fusion.131
  186.1 4.1 copy.127
  190.2 5.1 fusion.133
  195.3 4.1 copy.128
  199.4 4.5 constant_dynamic-update-slice_fusion.3
  210.1 4.1 fusion.130
  214.1 5.2 fusion.131
  222.9 4.1 copy.127
  227.1 5.1 fusion.133
  232.1 4.1 copy.128
  236.3 4.5 constant_dynamic-update-slice_fusion.3
  249.1 4.1 fusion.52
  253.2 39.1 %reduce-scatter.5.cloned.1.call-done = bf16[4,128,512]{2,1,0:T(8,128)(2,1)} async-done(((bf16[4,1024,512]{2,1,0:T(8,128)(2,1)}), bf16[4,128,512]{2,1,0:T(8,128)(2,1)}) %reduce-scatter.5.cloned.1.call-update) | async-done | bytes 524304 | tf_op jit(solution)/shard_map/reduce_scatter | solution.py:200
  294.4 53.5 %reduce-scatter.3.cloned.1.call-done = bf16[4,128,512]{2,1,0:T(8,128)(2,1)} async-done(((bf16[4,1024,512]{2,1,0:T(8,128)(2,1)}), bf16[4,128,512]{2,1,0:T(8,128)(2,1)}) %reduce-scatter.3.cloned.1.call-update) | async-done | bytes 524304 | tf_op jit(solution)/shard_map/reduce_scatter | solution.py:197
  349.9 3.9 fusion.37
  355.2 4.8 fusion.32
  362.5 41.6 %all-reduce = (f32[512]{0:T(512)}, f32[512]{0:T(512)}, f32[512]{0:T(512)}, f32[512]{0:T(512)}, f32[512]{0:T(512)}, /*index=5*/f32[512]{0:T(512)}, f32[512]{0:T(512)}, f32[2048]{0:T(1024)}, f32[512]{0:T(512)}) all-reduce(f32[512]{0:T(512)S(1)} %get-tuple-element.301, ...), channel_id=1, replica_groups=mesh['seq'=8,'row'=4] {'seq','row'}, use_global_device_ids=true, to_apply=%region_18.19 | all-reduce | flops 6144 | bytes 49152 | tf_op jit(solution)/shard_map/psum | solution.py:216
  406.9 180.9 %all-reduce.4.cloned.1.call-done = (f32[512,1536]{1,0:T(8,128)}, f32[512,512]{1,0:T(8,128)}, f32[512,2048]{1,0:T(8,128)}, f32[2048,512]{1,0:T(8,128)}) async-done(((f32[512,1536]{1,0:T(8,128)}, f32[512,512]{1,0:T(8,128)}, f32[512,2048]{1,0:T(8,128)}, f32[2048,512]{1,0:T(8,128)}), (f32[512,1536]{1,0:T(8,128)}, f32[512,512]{1,0:T(8,128)}, f32[512,2048]{1,0:T(8,128)}, ...) | async-done | bytes 12582928 | tf_op jit(solution)/shard_map/psum | solution.py:216
  587.9 3.9 copy.159
  (236 shorter events, 89.7 us)
Async XLA Ops:
  7.2 138.8 %copy-start = (bf16[2048,512]{1,0:T(8,128)(2,1)S(1)}, bf16[2048,512]{1,0:T(8,128)(2,1)}, u32[]{:S(2)}) copy-start(bf16[2048,512]{1,0:T(8,128)(2,1)} %param.33) | copy-start | bytes 6291460
  7.2 50.9 %all-gather.3.cloned.1.call-start = ((), (), s32[]{:S(2)}) async-start(), calls=%async_computation.2 | async-start | bytes 4718592 | tf_op jit(solution)/shard_map/all_gather | solution.py:86
  12.4 5.4 copy-start.58
  12.4 5.4 copy-start.59
  17.8 6.5 %copy-start.38 = (s32[4,1024]{1,0:T(4,128)S(1)}, s32[4,1024]{1,0:T(4,128)}, u32[]{:S(2)}) copy-start(s32[4,1024]{1,0:T(4,128)} %param.21) | copy-start | bytes 49156
  17.8 80.2 %all-gather.5.cloned.1.call-start = ((), (), s32[]{:S(2)}) async-start(), calls=%async_computation.3 | async-start | bytes 4718592 | tf_op jit(solution)/shard_map/all_gather | solution.py:87
  20.7 271.6 %reduce-scatter.5.cloned.1.call-start = ((), (), s32[]{:S(2)}) async-start(), calls=%async_computation.5 | async-start | bytes 4718592 | tf_op jit(solution)/shard_map/reduce_scatter | solution.py:200
  98.0 44.5 %copy-start.10 = (bf16[4,128,512]{2,1,0:T(8,128)(2,1)S(1)}, bf16[4,128,512]{2,1,0:T(8,128)(2,1)}, u32[]{:S(2)}) copy-start(bf16[4,128,512]{2,1,0:T(8,128)(2,1)} %param.20) | copy-start | bytes 1572868
  98.0 44.5 %copy-start.64 = (f32[512]{0:T(512)S(1)}, f32[512]{0:T(512)}, u32[]{:S(2)}) copy-start(f32[512]{0:T(512)} %param.28) | copy-start | bytes 6148
  108.4 5.8 copy-start.1
  129.5 5.8 copy-start.1
  144.3 8.2 %copy-start.7 = (f32[512,512]{1,0:T(8,128)}, f32[512,512]{1,0:T(8,128)S(1)}, u32[]{:S(2)}) copy-start(f32[512,512]{1,0:T(8,128)S(1)} %get-tuple-element.388) | copy-start | bytes 3145732
  144.3 8.2 %copy-start.39 = (f32[512]{0:T(512)}, f32[512]{0:T(512)S(1)}, u32[]{:S(2)}) copy-start(f32[512]{0:T(512)S(1)} %broadcast_multiply_fusion) | copy-start | bytes 6148
  144.6 7.9 %copy-start.41 = (f32[512]{0:T(512)}, f32[512]{0:T(512)S(1)}, u32[]{:S(2)}) copy-start(f32[512]{0:T(512)S(1)} %fusion.44) | copy-start | bytes 6148
  177.6 5.6 copy-start.3
  214.1 5.9 copy-start.3
  240.8 107.0 %reduce-scatter.3.cloned.1.call-start = ((), (), s32[]{:S(2)}) async-start(), calls=%async_computation.4 | async-start | bytes 4718592 | tf_op jit(solution)/shard_map/reduce_scatter | solution.py:197
  241.4 346.5 %all-reduce.4.cloned.1.call-start = ((), (), s32[]{:S(2)}) async-start(), calls=%async_computation.6 | async-start | bytes 25165824 | tf_op jit(solution)/shard_map/psum | solution.py:216
  242.7 107.2 %copy-start.34 = (bf16[64,8,4,128]{3,1,2,0:T(8,128)(2,1)}, bf16[64,8,4,128]{3,1,2,0:T(8,128)(2,1)S(1)}, u32[]{:S(2)}) copy-start(bf16[64,8,4,128]{3,1,2,0:T(8,128)(2,1)S(1)} %copy.124) | copy-start | bytes 1572868
  249.1 100.8 %copy-start.25 = (bf16[512,512]{1,0:T(8,128)(2,1)S(1)}, bf16[512,512]{1,0:T(8,128)(2,1)}, u32[]{:S(2)}) copy-start(bf16[512,512]{1,0:T(8,128)(2,1)} %copy-done.24) | copy-start | bytes 1572868
  355.2 4.9 copy-start.27
  355.2 5.0 copy-start.11
  355.2 5.0 copy-start.31
  355.2 5.0 copy-start.35
  355.2 5.0 copy-start.36
  355.2 5.0 copy-start.37
  355.2 5.0 copy-start.48
  355.2 5.0 copy-start.51
  360.3 43.8 %copy-start.12 = (bf16[4,128,512]{2,1,0:T(8,128)(2,1)S(1)}, bf16[4,128,512]{2,1,0:T(8,128)(2,1)}, u32[]{:S(2)}) copy-start(bf16[4,128,512]{2,1,0:T(8,128)(2,1)} %param.20) | copy-start | bytes 1572868
  360.3 43.8 %copy-start.18 = (bf16[4,128,512]{2,1,0:T(8,128)(2,1)S(1)}, bf16[4,128,512]{2,1,0:T(8,128)(2,1)}, u32[]{:S(2)}) copy-start(bf16[4,128,512]{2,1,0:T(8,128)(2,1)} %param.35) | copy-start | bytes 1572868
  360.3 43.8 %copy-start.55 = (f32[512]{0:T(512)S(1)}, f32[512]{0:T(512)}, u32[]{:S(2)}) copy-start(f32[512]{0:T(512)} %copy-done.54) | copy-start | bytes 6148
  587.9 4.9 copy-start.22
  (44 other events, 121.1 us)
Sparse Core Ops, SparseCore 0:
  17.9 40.1 all-gather.2
  60.5 37.4 all-gather.4
  240.9 51.3 reduce-scatter.4
  296.5 51.3 reduce-scatter.2
  354.7 233.1 all-reduce.3
where the time goes:
time: 609 us; the launch traced here: 605 us
  waiting for transfers between devices  348 us (57%)
  matrix products  91.7 us (15%)
  local copies, waits for them, and re-layouts  77.4 us (13%)
  blocking collectives  41.6 us (7%)
  other arithmetic  28.5 us (5%)
  between operations  15 us (2%)
    psum x1, waiting for transfers between devices, per_device(): lax.psum((grad_ln1_gain, grad_ln1_shift, grad_w_qkv, grad_bias_query, gra...  181 us
    reduce_scatter x1, waiting for transfers between devices, per_device(): lax.psum_scatter(key_terms.astype(jnp.bfloat16), 'seq', scatter_dimension...  53.5 us
    psum x1, blocking collectives, per_device(): lax.psum((grad_ln1_gain, grad_ln1_shift, grad_w_qkv, grad_bias_query, gra...  41.6 us
    all_gather x1, waiting for transfers between devices, per_device(): lax.all_gather(values_band, 'seq', axis=1, tiled=True)  39.9 us
    reduce_scatter x1, waiting for transfers between devices, per_device(): lax.psum_scatter(value_terms.astype(jnp.bfloat16), 'seq', scatter_dimensi...  39.1 us
    all_gather x1, waiting for transfers between devices, per_device(): lax.all_gather(keys_band, 'seq', axis=1, tiled=True)  33.8 us
    unnamed x130, local copies, waits for them, and re-layouts  19.1 us
    dynamic_update_slice x4, local copies, waits for them, and re-layouts, local_grads(): lax.dynamic_update_slice_in_dim(value_buffer, grad_value.reshape(row_coun...  17.3 us
  transfers between devices with their start and end apart: 5, of which 5 were waited for; matrix products, arithmetic and copies ran while one was open for 5% of the time, Pallas kernels for 0%

commit v1 on v0

v1 whole, which is shorter than its diff:
```python
import functools

import jax
import jax.numpy as jnp
from jax import lax
from jax.experimental import pallas as pl
from jax.experimental.pallas import tpu as pltpu
from jax.sharding import PartitionSpec as P

HEADS = 8
EPSILON = 1e-06
BIG = 1e30
LSE_LANE = 16
F32 = jnp.float32
BF16 = jnp.bfloat16
VMEM_LIMIT = 48 * 1024 * 1024


def dot_nn(a, b):
    return lax.dot_general(a, b, (((1,), (0,)), ((), ())), preferred_element_type=F32)


def dot_nt(a, b):
    return lax.dot_general(a, b, (((1,), (1,)), ((), ())), preferred_element_type=F32)


def dot_tn(a, b):
    return lax.dot_general(a, b, (((0,), (0,)), ((), ())), preferred_element_type=F32)


def split_three(value):
    high = value.astype(BF16)
    rest = value - high.astype(F32)
    middle = rest.astype(BF16)
    low = (rest - middle.astype(F32)).astype(BF16)
    return high, middle, low


def lane_index(shape):
    return lax.broadcasted_iota(jnp.int32, shape, len(shape) - 1)


def three_lanes(value, lanes):
    high, middle, low = split_three(value)
    spot = lanes % 64
    out = jnp.where(spot == LSE_LANE, high.astype(F32), 0.0)
    out = jnp.where(spot == LSE_LANE + 1, middle.astype(F32), out)
    return jnp.where(spot == LSE_LANE + 2, low.astype(F32), out)


def norm_parts(value):
    centre = jnp.mean(value, axis=-1, keepdims=True)
    centred = value - centre
    spread = jnp.mean(centred * centred, axis=-1, keepdims=True)
    scale = lax.rsqrt(spread + EPSILON)
    return centred * scale, scale


def norm_back(grad, unit, scale, gain):
    grad_unit = grad * gain
    first = jnp.mean(grad_unit, axis=-1, keepdims=True)
    second = jnp.mean(grad_unit * unit, axis=-1, keepdims=True)
    return scale * (grad_unit - first - unit * second)


def qkv_kernel(pieces, width, *refs):
    x_refs = refs[:pieces]
    gain, shift, w_ref, bq_ref, bv_ref, normed_ref, q_ref, kv_ref = refs[pieces:]
    band = x_refs[0].shape[0]
    for j in range(pieces):
        unit, _ = norm_parts(x_refs[j][...].astype(F32))
        normed_ref[j * band : (j + 1) * band, :] = (unit * gain[...] + shift[...]).astype(BF16)
    normed = normed_ref[...]
    q = dot_nn(normed, w_ref[:, :width])
    q_ref[...] = ((q + bq_ref[...]) * (width // HEADS) ** -0.5).astype(BF16)
    kv_ref[:, :width] = dot_nn(normed, w_ref[:, width : 2 * width]).astype(BF16)
    kv_ref[:, width:] = (dot_nn(normed, w_ref[:, 2 * width :]) + bv_ref[...]).astype(BF16)


def forward_kernel(parts, rows, *refs):
    q_ref = refs[0]
    k_refs = refs[1 : 1 + parts]
    v_refs = refs[1 + parts : 1 + 2 * parts]
    qf_ref, kf_ref, mix_ref, qfb_ref, k_aug, v_aug = refs[1 + 2 * parts :]
    tokens = q_ref.shape[0]
    low_half = (lane_index((1, 128)) < 64).astype(F32)
    halves = (low_half.astype(BF16), (1.0 - low_half).astype(BF16))
    for parity in range(2):
        mine, other = halves[parity], halves[1 - parity]
        start = 0
        for k_ref, v_ref in zip(k_refs, v_refs):
            stop = start + k_ref.shape[0]
            k_aug[parity, start:stop, :] = k_ref[...] * mine + kf_ref[start:stop, :] * other
            v_aug[parity, start:stop, :] = v_ref[...] * mine + other
            start = stop
    lanes = lane_index((rows, 128))
    low = lanes < 64

    def block(step, carry):
        at = pl.ds(pl.multiple_of(step * rows, rows), rows)
        q = q_ref[at, :]
        qf = qf_ref[at, :]
        sums, tops = [], []
        for parity in range(2):
            mine, other = halves[parity], halves[1 - parity]
            scores = dot_nt(q * mine + qf * other, k_aug[parity])
            top = jnp.max(scores, axis=-1, keepdims=True)
            exps = jnp.exp(scores - top).astype(BF16)
            sums.append(dot_nn(exps, v_aug[parity]))
            tops.append(jnp.broadcast_to(top, (rows, 128)))
        total = jnp.where(low, sums[1], sums[0])
        mix_ref[at, :] = jnp.where(low, sums[0], sums[1]) / pltpu.roll(total, 64, 1)
        log_total = jnp.where(low, tops[1], tops[0]) + jnp.log(total)
        qfb_ref[at, :] = (qf.astype(F32) + three_lanes(-log_total, lanes)).astype(BF16)
        return carry

    lax.fori_loop(0, tokens // rows, block, 0)


def attention_forward(q, kvs, qf, kf, rows=256):
    tokens, width = q.shape
    pairs = width // 128
    length = kf.shape[0]
    parts = len(kvs)
    in_specs = [pl.BlockSpec((tokens, 128), lambda h: (0, h))]
    in_specs += [pl.BlockSpec((kv.shape[0], 128), lambda h: (0, h)) for kv in kvs]
    in_specs += [pl.BlockSpec((kv.shape[0], 128), lambda h: (0, pairs + h)) for kv in kvs]
    in_specs += [
        pl.BlockSpec((tokens, 128), lambda h: (0, 0)),
        pl.BlockSpec((length, 128), lambda h: (0, 0)),
    ]
    return pl.pallas_call(
        functools.partial(forward_kernel, parts, rows),
        grid=(pairs,),
        in_specs=in_specs,
        out_specs=[
            pl.BlockSpec((tokens, 128), lambda h: (0, h)),
            pl.BlockSpec((tokens, 128), lambda h: (0, h)),
        ],
        out_shape=[
            jax.ShapeDtypeStruct((tokens, width), F32),
            jax.ShapeDtypeStruct((tokens, width), BF16),
        ],
        scratch_shapes=[pltpu.VMEM((2, length, 128), BF16), pltpu.VMEM((2, length, 128), BF16)],
        compiler_params=pltpu.CompilerParams(vmem_limit_bytes=VMEM_LIMIT),
        name="attention_forward",
        cost_estimate=pl.CostEstimate(
            flops=4 * tokens * length * width, bytes_accessed=8 * tokens * width,
            transcendentals=tokens * length * HEADS,
        ),
    )(q, *kvs, *kvs, qf, kf)


def backward_kernel(parts, rows, *refs):
    q_ref, gm_ref, qfb_ref, gmf_ref = refs[:4]
    k_refs = refs[4 : 4 + parts]
    v_refs = refs[4 + parts : 4 + 2 * parts]
    kf_ref = refs[4 + 2 * parts]
    rest = refs[5 + 2 * parts :]
    dq_ref = rest[0]
    dk_refs = rest[1 : 1 + parts]
    dv_refs = rest[1 + parts : 1 + 2 * parts]
    q_aug, gm_aug, dqt = rest[1 + 2 * parts :]
    low_half = (lane_index((1, 128)) < 64).astype(F32)
    halves = (low_half.astype(BF16), (1.0 - low_half).astype(BF16))
    for parity in range(2):
        mine, other = halves[parity], halves[1 - parity]
        q_aug[parity] = q_ref[...] * mine + qfb_ref[...] * other
        gm_aug[parity] = gm_ref[...] * mine + gmf_ref[...] * other
    dqt[...] = jnp.zeros_like(dqt)
    low = lane_index((rows, 128)) < 64
    start = 0
    for k_ref, v_ref, dk_ref, dv_ref in zip(k_refs, v_refs, dk_refs, dv_refs):

        def block(step, carry, start=start, k_ref=k_ref, v_ref=v_ref, dk_ref=dk_ref, dv_ref=dv_ref):
            at = pl.ds(pl.multiple_of(step * rows, rows), rows)
            at_all = pl.ds(pl.multiple_of(start + step * rows, rows), rows)
            k, v, kf = k_ref[at, :], v_ref[at, :], kf_ref[at_all, :]
            dks, dvs = [], []
            for parity in range(2):
                mine, other = halves[parity], halves[1 - parity]
                k_aug = k * mine + kf * other
                v_aug = v * mine + other
                probs = jnp.exp(dot_nt(k_aug, q_aug[parity]))
                slopes = dot_nt(v_aug, gm_aug[parity])
                grads = (probs * slopes).astype(BF16)
                dvs.append(dot_nn(probs.astype(BF16), gm_ref[...]))
                dks.append(dot_nn(grads, q_ref[...]))
                dqt[parity] += dot_tn(k, grads)
            dk_ref[at, :] = jnp.where(low, dks[0], dks[1]).astype(dk_ref.dtype)
            dv_ref[at, :] = jnp.where(low, dvs[0], dvs[1]).astype(dv_ref.dtype)
            return carry

        lax.fori_loop(0, k_ref.shape[0] // rows, block, 0)
        start += k_ref.shape[0]
    dq_t = jnp.concatenate([dqt[0, :64, :], dqt[1, 64:, :]], axis=0)
    dq_ref[...] = dq_t.T.astype(BF16) * (64.0**-0.5)


def attention_backward(q, gm, qfb, gmf, kvs, kf, first, count, rows=256):
    tokens, width = q.shape
    pairs = width // 128
    length = kf.shape[0]
    parts = len(kvs)
    of_pair = lambda h: (0, first + h)
    in_specs = [pl.BlockSpec((tokens, 128), of_pair)] * 4
    in_specs += [pl.BlockSpec((kv.shape[0], 128), of_pair) for kv in kvs]
    in_specs += [pl.BlockSpec((kv.shape[0], 128), lambda h: (0, pairs + first + h)) for kv in kvs]
    in_specs += [pl.BlockSpec((length, 128), lambda h: (0, 0))]
    kinds = [F32] + [BF16] * (parts - 1)
    wide = 128 * count
    outs = [jax.ShapeDtypeStruct((tokens, wide), BF16)]
    outs += [jax.ShapeDtypeStruct((kv.shape[0], wide), kind) for kv, kind in zip(kvs, kinds)] * 2
    out_specs = [pl.BlockSpec((tokens, 128), lambda h: (0, h))]
    out_specs += [pl.BlockSpec((kv.shape[0], 128), lambda h: (0, h)) for kv in kvs] * 2
    got = pl.pallas_call(
        functools.partial(backward_kernel, parts, rows),
        grid=(count,),
        in_specs=in_specs,
        out_specs=out_specs,
        out_shape=outs,
        scratch_shapes=[
            pltpu.VMEM((2, tokens, 128), BF16),
            pltpu.VMEM((2, tokens, 128), BF16),
            pltpu.VMEM((2, 128, tokens), F32),
        ],
        compiler_params=pltpu.CompilerParams(vmem_limit_bytes=VMEM_LIMIT),
        name="attention_backward",
        cost_estimate=pl.CostEstimate(
            flops=10 * tokens * length * wide, bytes_accessed=12 * tokens * wide,
            transcendentals=tokens * length * wide // 64,
        ),
    )(q, gm, qfb, gmf, *kvs, *kvs, kf)
    return got[0], got[1 : 1 + parts], got[1 + parts :]


def middle_kernel(pieces, rows, *refs):
    x_refs = refs[:pieces]
    dy_refs = refs[pieces : 2 * pieces]
    (mix_ref, w_out, b_out, gain, shift, w_up, b_up, w_down, b_down) = refs[2 * pieces : 2 * pieces + 9]
    outs = refs[2 * pieces + 9 :]
    (out_ref, mixed_ref, two_ref, active_ref, gh_ref, ga_ref, gmid_ref, gm_ref, gmf_ref, vec_ref, dy_ref) = outs
    band = x_refs[0].shape[0]
    tokens, width = mix_ref.shape
    ff = w_up.shape[1]
    vec_ref[...] = jnp.zeros_like(vec_ref)
    c0 = 0.7978845608028654
    c1 = 0.044715
    row = lax.broadcasted_iota(jnp.int32, (width, width), 0) // 64
    column = lane_index((width, width)) // 64
    opposite = (row == (column + 1 - 2 * (column % 2))).astype(F32).astype(BF16)
    per = rows // band
    for t in range(tokens // rows):
        at = slice(t * rows, (t + 1) * rows)
        x = jnp.concatenate([x_refs[t * per + j][...] for j in range(per)], axis=0).astype(F32)
        dy = jnp.concatenate([dy_refs[t * per + j][...] for j in range(per)], axis=0)
        dy_ref[at, :] = dy
        mix = mix_ref[at, :]
        mixed = mix.astype(BF16)
        mixed_ref[at, :] = mixed
        middle = x + (dot_nn(mixed, w_out[...]) + b_out[...])
        unit, scale = norm_parts(middle)
        two = (unit * gain[...] + shift[...]).astype(BF16)
        two_ref[at, :] = two
        out = middle + b_down[...]
        grad_two = jnp.zeros((rows, width), F32)
        step = 512
        for f in range(0, ff, step):
            fs = slice(f, f + step)
            hidden = dot_nn(two, w_up[:, fs]) + b_up[:, fs]
            square = hidden * hidden
            tanh = jnp.tanh(c0 * hidden * (1.0 + c1 * square))
            half = 0.5 * (1.0 + tanh)
            active = (hidden * half).astype(BF16)
            active_ref[at, fs] = active
            out = out + dot_nn(active, w_down[fs, :])
            slope = half + hidden * (0.5 * (1.0 - tanh * tanh)) * (c0 + (3.0 * c0 * c1) * square)
            grad = dot_nt(dy, w_down[fs, :]) * slope
            grad_low = grad.astype(BF16)
            gh_ref[at, fs] = grad_low
            vec_ref[0:1, fs] += jnp.sum(grad_low.astype(F32), axis=0, keepdims=True)
            grad_two = grad_two + dot_nt(grad_low, w_up[:, fs])
        out_ref[at, :] = out.astype(BF16)
        dy_wide = dy.astype(F32)
        grad_middle = dy_wide + norm_back(grad_two, unit, scale, gain[...])
        gmid_ref[at, :] = grad_middle
        vec_ref[1:2, :width] += jnp.sum(grad_two * unit, axis=0, keepdims=True)
        vec_ref[2:3, :width] += jnp.sum(grad_two, axis=0, keepdims=True)
        vec_ref[3:4, :width] += jnp.sum(dy_wide, axis=0, keepdims=True)
        grad_attn = grad_middle.astype(BF16)
        ga_ref[at, :] = grad_attn
        vec_ref[4:5, :width] += jnp.sum(grad_attn.astype(F32), axis=0, keepdims=True)
        gm = dot_nt(grad_attn, w_out[...]).astype(BF16)
        gm_ref[at, :] = gm
        high, mid, low = split_three(gm.astype(F32) * mix)
        inner = dot_nn(high, opposite) + (dot_nn(mid, opposite) + dot_nn(low, opposite))
        gmf_ref[at, :] = three_lanes(-inner, lane_index((rows, width))).astype(BF16)


def middle_part(xs, dys, mix, w_out, b_out, gain, shift, w_up, b_up, w_down, b_down, rows=256):
    tokens, width = mix.shape
    ff = w_up.shape[1]
    shape = jax.ShapeDtypeStruct
    return pl.pallas_call(
        functools.partial(middle_kernel, len(xs), rows),
        out_shape=[
            shape((tokens, width), BF16),
            shape((tokens, width), BF16),
            shape((tokens, width), BF16),
            shape((tokens, ff), BF16),
            shape((tokens, ff), BF16),
            shape((tokens, width), BF16),
            shape((tokens, width), F32),
            shape((tokens, width), BF16),
            shape((tokens, width), BF16),
            shape((8, ff), F32),
            shape((tokens, width), BF16),
        ],
        compiler_params=pltpu.CompilerParams(vmem_limit_bytes=VMEM_LIMIT),
        name="middle_part",
        cost_estimate=pl.CostEstimate(
            flops=2 * tokens * width * (4 * ff + 5 * width), bytes_accessed=8 * 1024 * 1024,
            transcendentals=tokens * ff,
        ),
    )(*xs, *dys, mix, w_out, b_out, gain, shift, w_up, b_up, w_down, b_down)


def last_kernel(pieces, *refs):
    x_refs = refs[:pieces]
    dq_ref, dk_ref, dv_ref, gmid_ref, gain, w_ref = refs[pieces : pieces + 6]
    out_ref, vec_ref = refs[pieces + 6 :]
    width = dq_ref.shape[1]
    grad = dot_nt(dq_ref[...], w_ref[:, :width])
    grad = grad + dot_nt(dk_ref[...], w_ref[:, width : 2 * width])
    grad = grad + dot_nt(dv_ref[...], w_ref[:, 2 * width :])
    x = jnp.concatenate([ref[...] for ref in x_refs], axis=0).astype(F32)
    unit, scale = norm_parts(x)
    out_ref[...] = (gmid_ref[...] + norm_back(grad, unit, scale, gain[...])).astype(BF16)
    vec_ref[...] = jnp.zeros_like(vec_ref)
    vec_ref[0:1, :] = jnp.sum(dq_ref[...].astype(F32), axis=0, keepdims=True)
    vec_ref[1:2, :] = jnp.sum(dv_ref[...].astype(F32), axis=0, keepdims=True)
    vec_ref[2:3, :] = jnp.sum(grad * unit, axis=0, keepdims=True)
    vec_ref[3:4, :] = jnp.sum(grad, axis=0, keepdims=True)


def swap(value, axis, size, mask):
    return lax.ppermute(value, axis, [(i, i ^ mask) for i in range(size)])


def scatter_sum(value, bits):
    for axis, size, mask, own in bits:
        half = value.shape[0] // 2
        sent = lax.dynamic_slice_in_dim(value, (1 - own) * half, half, 0)
        kept = lax.dynamic_slice_in_dim(value, own * half, half, 0)
        got = swap(sent, axis, size, mask)
        value = (kept.astype(F32) + got.astype(F32)).astype(BF16)
    return value


def gather_back(value, bits):
    for axis, size, mask, own in reversed(bits):
        got = swap(value, axis, size, mask)
        value = jnp.where(
            own == 0, jnp.concatenate([value, got], 0), jnp.concatenate([got, value], 0)
        )
    return value


def exchange_sum(value, bits):
    for axis, size, mask, own in bits:
        value = (value.astype(F32) + swap(value, axis, size, mask).astype(F32)).astype(value.dtype)
    return value


def bits_of(axis, size):
    found, mask = [], 1
    while mask < size:
        found.append((axis, size, mask, (lax.axis_index(axis) // mask) % 2))
        mask *= 2
    return found


def per_device(
    seq_size, row_size,
    block_input, segment_ids, ln1_gain, ln1_shift, w_qkv, bias_query, bias_value, w_out, bias_out,
    ln2_gain, ln2_shift, w_up, bias_up, w_down, bias_down, out_grad,
):
    rows, band, width = block_input.shape
    length = segment_ids.shape[1]
    share = seq_size // rows
    tokens = rows * band
    crops = max(length // (4 * band), 1)
    place = lax.axis_index("seq")
    my_row, my_part = place // share, place % share

    def deal(pieces):
        got = [pieces[0]]
        for j in range(1, rows):
            turn = [(s, ((s // share) ^ j) * share + s % share) for s in range(seq_size)]
            got.append(lax.ppermute(pieces[j], "seq", turn))
        return got

    def pick(array):
        return [lax.dynamic_index_in_dim(array, my_row ^ j, 0, False) for j in range(rows)]

    xs = deal(pick(block_input))
    dys = deal(pick(out_grad))

    own_row = lax.dynamic_index_in_dim(segment_ids, my_row, 0, False).reshape(seq_size, band)
    key_ids = jnp.concatenate(
        [
            lax.dynamic_index_in_dim(own_row, (my_row ^ j) * share + (my_part ^ i), 0, False)
            for i in range(share)
            for j in range(rows)
        ]
    )
    spot = jnp.arange(128) % 64
    same = key_ids[:, None] == spot[None, :]
    used = spot[None, :] < crops
    ones = (spot >= LSE_LANE) & (spot < LSE_LANE + 3)
    kf = jnp.where(used, jnp.where(same, 0.0, -1.0), jnp.where(ones, 1.0, 0.0)).astype(BF16)
    qf = jnp.where(used & same, BIG, 0.0).astype(BF16)[:tokens]

    row_of = lambda v: v.reshape(1, -1)
    shape = jax.ShapeDtypeStruct
    normed, q, kv = pl.pallas_call(
        functools.partial(qkv_kernel, rows, width),
        out_shape=[
            shape((tokens, width), BF16),
            shape((tokens, width), BF16),
            shape((tokens, 2 * width), BF16),
        ],
        compiler_params=pltpu.CompilerParams(vmem_limit_bytes=VMEM_LIMIT),
        name="norm_and_project",
    )(*xs, row_of(ln1_gain), row_of(ln1_shift), w_qkv, row_of(bias_query), row_of(bias_value))

    seq_bits = bits_of("seq", seq_size)
    row_bits = bits_of("row", row_size)
    part_bits = [bit for bit in seq_bits if bit[2] < share]
    kvs, whole = [kv], kv
    for axis, size, mask, own in part_bits:
        got = swap(whole, axis, size, mask)
        kvs.append(got)
        if mask * 2 < share:
            whole = jnp.concatenate([whole, got], 0)

    mix, qfb = attention_forward(q, kvs, qf, kf)
    (out, mixed, two, active, grad_hidden, grad_attn, grad_middle, gm, gmf, vec, dy) = middle_part(
        xs, dys, mix, w_out, row_of(bias_out), row_of(ln2_gain), row_of(ln2_shift),
        w_up, row_of(bias_up), w_down, row_of(bias_down),
    )

    bits = seq_bits + row_bits
    cut, rest = bits[:5], bits[5:]
    turned = [cut[0], cut[2], cut[1]] + cut[3:]
    grad_down = dot_tn(active, dy).astype(BF16)
    grad_up_out = jnp.concatenate(
        [dot_tn(two, grad_hidden).astype(BF16), dot_tn(mixed, grad_attn).astype(BF16)], axis=1
    )

    dq, dks, dvs = attention_backward(q, gm, qfb, gmf, kvs, kf, 0, width // 128)

    if share == 2:
        axis, size, mask, own = part_bits[0]
        got = swap(jnp.concatenate([dks[1], dvs[1]], axis=1), axis, size, mask)
        dk = (dks[0] + got[:, :width].astype(F32)).astype(BF16)
        dv = (dvs[0] + got[:, width:].astype(F32)).astype(BF16)
    else:
        both = jnp.concatenate(
            [jnp.concatenate([part.astype(BF16) for part in terms], 0) for terms in (dks, dvs)], axis=1
        )
        for axis, size, mask, own in reversed(part_bits):
            half = both.shape[0] // 2
            both = (both[:half].astype(F32) + swap(both[half:], axis, size, mask).astype(F32)).astype(BF16)
        dk, dv = both[:, :width], both[:, width:]

    grad_w_qkv = jnp.concatenate([dot_tn(normed, part).astype(BF16) for part in (dq, dk, dv)], axis=1)

    input_grad, vec_last = pl.pallas_call(
        functools.partial(last_kernel, rows),
        out_shape=[shape((tokens, width), BF16), shape((8, width), F32)],
        compiler_params=pltpu.CompilerParams(vmem_limit_bytes=VMEM_LIMIT),
        name="norm_one_back",
    )(*xs, dq, dk, dv, grad_middle, row_of(ln1_gain), w_qkv)

    def reduce_all(value, order):
        return gather_back(exchange_sum(scatter_sum(value, order), rest), order).astype(F32)

    def back(value):
        got = deal([value[j * band : (j + 1) * band] for j in range(rows)])
        stacked = jnp.stack(got)
        return jnp.stack([lax.dynamic_index_in_dim(stacked, my_row ^ j, 0, False) for j in range(rows)])

    sum_down = reduce_all(grad_down, cut)
    sum_up_out = reduce_all(grad_up_out, turned)
    sum_qkv = reduce_all(grad_w_qkv, cut)
    ff = w_up.shape[1]
    vectors = jnp.concatenate([vec[0], vec[1:5, :width].reshape(-1), vec_last[:4].reshape(-1)])
    vectors = exchange_sum(vectors.reshape(-1, 512), bits).reshape(-1)
    cuts = [ff + i * width for i in range(9)]
    bias_up_sum = vectors[:ff]
    ln2_gain_sum, ln2_shift_sum, bias_down_sum, bias_out_sum, bias_q_sum, bias_v_sum, ln1_gain_sum, ln1_shift_sum = [
        vectors[a:b] for a, b in zip(cuts[:-1], cuts[1:])
    ]
    return (
        back(out),
        back(input_grad),
        ln1_gain_sum,
        ln1_shift_sum,
        sum_qkv,
        bias_q_sum,
        bias_v_sum,
        sum_up_out[:, ff:],
        bias_out_sum,
        ln2_gain_sum,
        ln2_shift_sum,
        sum_up_out[:, :ff],
        bias_up_sum,
        sum_down,
        bias_down_sum,
    )


def solution(mesh):
    split = P("row", "seq", None)
    placed = (split, P("row", None)) + (P(),) * 13 + (split,)
    return jax.shard_map(
        functools.partial(per_device, mesh.shape["seq"], mesh.shape["row"]),
        mesh=mesh,
        in_specs=placed,
        out_specs=(split, split) + (P(),) * 13,
        check_vma=False,
    )
```

time: 609 us -> 218 us (0.36)
  waiting for transfers between devices: 348 us -> 70.8 us
  matrix products: 91.7 us -> 7.13 us
  local copies, waits for them, and re-layouts: 77.4 us -> 14.2 us
  starting transfers between devices: 0.63 us -> 60.4 us
  Pallas kernels: 0 us -> 45.4 us
  blocking collectives: 41.6 us -> 0 us
  between operations: 15 us -> 1.95 us
  other arithmetic: 28.5 us -> 17.5 us
    psum x1 -> x0, waiting for transfers between devices: 181 us -> none  [per_device(): lax.psum((grad_ln1_gain, grad_ln1_shift, grad_w_qkv, grad_bias_query, gra...]
    reduce_scatter x2 -> x0, waiting for transfers between devices: 92.5 us -> none  [the longest x1 53.5 us: per_device(): lax.psum_scatter(key_terms.astype(jnp.bfloat16), 'seq', scatter_dimension...]
    dot_general x26 -> x6, matrix products: 91.7 us -> 7.13 us  [dot_tn(): lax.dot_general(a, b, (((0,), (0,)), ((), ())), preferred_element_type=F32)]
    all_gather x2 -> x0, waiting for transfers between devices: 73.7 us -> none  [the longest x1 39.9 us: per_device(): lax.all_gather(values_band, 'seq', axis=1, tiled=True)]
    ppermute x0 -> x49, waiting for transfers between devices: none -> 70.8 us  [the longest x37 69.5 us: swap(): return lax.ppermute(value, axis, [(i, i ^ mask) for i in range(size)])]
    ppermute x0 -> x49, starting transfers between devices: none -> 60.4 us  [the longest x37 43.8 us: swap(): return lax.ppermute(value, axis, [(i, i ^ mask) for i in range(size)])]
    pallas_call x0 -> x5, Pallas kernels: none -> 45.4 us  [the longest x1 15.9 us: attention_backward(): pl.pallas_call(functools.partial(backward_kernel, parts, rows), grid=(cou...]
    psum x1 -> x0, blocking collectives: 41.6 us -> none  [per_device(): lax.psum((grad_ln1_gain, grad_ln1_shift, grad_w_qkv, grad_bias_query, gra...]
  transfers between devices with their start and end apart: 5 -> 49, of which waited for: 5 -> 19; matrix products, arithmetic and copies ran while one was open for 5% -> 13% of each run, Pallas kernels for 0% -> 7%
where the time goes in v1:
time: 218 us; the launch traced here: 217 us
  waiting for transfers between devices  70.8 us (32%)
  starting transfers between devices  60.4 us (28%)
  Pallas kernels  45.4 us (21%)
  other arithmetic  17.5 us (8%)
  local copies, waits for them, and re-layouts  14.2 us (7%)
  matrix products  7.13 us (3%)
    ppermute x37, waiting for transfers between devices, swap(): return lax.ppermute(value, axis, [(i, i ^ mask) for i in range(size)])  69.5 us
    ppermute x37, starting transfers between devices, swap(): return lax.ppermute(value, axis, [(i, i ^ mask) for i in range(size)])  43.8 us
    ppermute x12, starting transfers between devices, deal(): got.append(lax.ppermute(pieces[j], 'seq', turn))  16.6 us
    pallas_call x1, Pallas kernels, attention_backward(): pl.pallas_call(functools.partial(backward_kernel, parts, rows), grid=(cou...  15.9 us
    pallas_call x1, Pallas kernels, middle_part(): pl.pallas_call(functools.partial(middle_kernel, len(xs), rows), out_shape...  13.7 us
    pallas_call x1, Pallas kernels, attention_forward(): pl.pallas_call(functools.partial(forward_kernel, parts, rows), grid=(pair...  11.9 us
    dot_general x6, matrix products, dot_tn(): lax.dot_general(a, b, (((0,), (0,)), ((), ())), preferred_element_type=F32)  7.13 us
    convert_element_type x3, other arithmetic, reduce_all(): gather_back(exchange_sum(scatter_sum(value, order), rest), order)  5.66 us
  transfers between devices with their start and end apart: 49, of which 19 were waited for; matrix products, arithmetic and copies ran while one was open for 13% of the time, Pallas kernels for 7%

profile of v1, /device:TPU:0, one launch (start us, length us, event | category | flops | bytes accessed | tf_op | source)
XLA Modules:
  0.0 217.3 jit_solution(951783835495580131)
XLA Ops:
  2.0 3.0 %collective-permute-start = (bf16[128,512]{1,0:T(8,128)(2,1)S(1)}, bf16[128,512]{1,0:T(8,128)(2,1)S(1)}, u32[]{:S(2)}, u32[]{:S(2)}) collective-permute-start(bf16[128,512]{1,0:T(8,128)(2,1)S(1)} %get-tuple-element.99), channel_id=1, source_target_pairs={{0,8},{4,12},{8,0},{12,4},{16,24},{20,28},{24,16},{28,20},{1,9},{5... | collective-permute-start | bytes 393224 | tf_op jit(solution)/shard_map/ppermute | solution.py:400
  13.6 2.3 %norm_and_project.1 = (bf16[512,512]{1,0:T(8,128)(2,1)S(1)}, bf16[512,512]{1,0:T(8,128)(2,1)S(1)}, bf16[512,1024]{1,0:T(8,128)(2,1)}) custom-call(bf16[128,512]{1,0:T(8,128)(2,1)S(1)} %get-tuple-element.100.refs_0_, bf16[128,512]{1,0:T(8,128)(2,1)S(1)} %collective-permute-done.refs_1_, bf16[128,512]{1,0:T(8,128)(2,1)S(1)} %collective-permute-done.1.refs_2_, ...), custom_call_target="tpu_custom_call" | custom-call | tf_op jit(solution)/shard_map/norm_and_project/pallas_call | solution.py:426
  19.8 11.9 %attention_forward.1 = (f32[512,512]{1,0:T(8,128)S(1)}, bf16[512,512]{1,0:T(8,128)(2,1)S(1)}) custom-call(bf16[512,512]{1,0:T(8,128)(2,1)S(1)} %get-tuple-element.38.refs_0_, bf16[512,1024]{1,0:T(8,128)(2,1)} %get-tuple-element.39.refs_1_.refs_3_.refs_4_.refs_6_, bf16[512,1024]{1,0:T(8,128)(2,1)} %collective-permute-done.6.refs_2_.refs_4_.refs_5_.refs_7_, ...), custom_call_target="tpu_custom_call" | custom-call | flops 1073741824 | bytes 2097152 | tf_op jit(solution)/shard_map/attention_forward/pallas_call | solution.py:132
  32.8 13.7 %middle_part.1 = (bf16[512,512]{1,0:T(8,128)(2,1)S(1)}, bf16[512,512]{1,0:T(8,128)(2,1)S(1)}, bf16[512,512]{1,0:T(8,128)(2,1)S(1)}, bf16[512,2048]{1,0:T(8,128)(...) custom-call(bf16[128,512]{1,0:T(8,128)(2,1)S(1)} %get-tuple-element., ...), custom_call_target="tpu_custom_call" | custom-call | flops 5637144576 | bytes 8388608 | tf_op jit(solution)/shard_map/middle_part/pallas_call | solution.py:304
  47.3 15.9 %attention_backward.1 = (bf16[512,512]{1,0:T(8,128)(2,1)S(1)}, f32[512,512]{1,0:T(8,128)S(1)}, bf16[512,512]{1,0:T(8,128)(2,1)S(1)}, f32[512,512]{1,0:T(8,128)S(1)}, bf16[512,512]{1,0:T(8,128)(2,1)S(1)}) custom-call(bf16[512,512]{1,0:T(8,128)(2,1)S(1)} %copy-done.19, bf16[512,512]{1,0:T(8,128)(2,1)S(1)} %get-tuple-element.42.refs_1_, ...), custom_call_target="tpu_custom_call" | custom-call | flops 2684354560 | bytes 3145728 | tf_op jit(solution)/shard_map/attention_backward/pallas_call | solution.py:216
  75.5 3.0 %convolution_convert_fusion = bf16[2048,512]{1,0:T(8,128)(2,1)S(1)} fusion(bf16[512,2048]{1,0:T(8,128)(2,1)} %get-tuple-element.59, bf16[512,512]{1,0:T(8,128)(2,1)} %copy-done.26), kind=kOutput, calls=%fused_computation.2 | convolution fusion | flops 1074790400 | bytes 4718592 | tf_op jit(solution)/shard_map/dot_general | solution.py:28
  89.3 3.2 %collective-permute-done.15 = f32[12,512]{1,0:T(8,128)S(1)} collective-permute-done((f32[12,512]{1,0:T(8,128)S(1)}, f32[12,512]{1,0:T(8,128)S(1)}, u32[]{:S(2)}, u32[]{:S(2)}) %collective-permute-start.15) | collective-permute-done | bytes 24608 | tf_op jit(solution)/shard_map/ppermute | solution.py:347
  93.3 3.1 %collective-permute-done.16 = f32[12,512]{1,0:T(8,128)S(1)} collective-permute-done((f32[12,512]{1,0:T(8,128)S(1)}, f32[12,512]{1,0:T(8,128)S(1)}, u32[]{:S(2)}, u32[]{:S(2)}) %collective-permute-start.16) | collective-permute-done | bytes 24608 | tf_op jit(solution)/shard_map/ppermute | solution.py:347
  100.5 2.4 %collective-permute-start.18 = (f32[12,512]{1,0:T(8,128)S(1)}, f32[12,512]{1,0:T(8,128)S(1)}, u32[]{:S(2)}, u32[]{:S(2)}) collective-permute-start(f32[12,512]{1,0:T(8,128)S(1)} %add.288), channel_id=1, source_target_pairs={{0,2},{1,3},{2,0},{3,1},{4,6},{5,7},{6,4},{7,5},{8,10},{9,11},{10,... | collective-permute-start | bytes 73736 | tf_op jit(solution)/shard_map/ppermute | solution.py:347
  103.0 2.3 %collective-permute-done.18 = f32[12,512]{1,0:T(8,128)S(1)} collective-permute-done((f32[12,512]{1,0:T(8,128)S(1)}, f32[12,512]{1,0:T(8,128)S(1)}, u32[]{:S(2)}, u32[]{:S(2)}) %collective-permute-start.18) | collective-permute-done | bytes 24608 | tf_op jit(solution)/shard_map/ppermute | solution.py:347
  107.0 10.3 %collective-permute-done.40 = bf16[512,512]{1,0:T(8,128)(2,1)S(1)} collective-permute-done((bf16[512,512]{1,0:T(8,128)(2,1)S(1)}, bf16[512,512]{1,0:T(8,128)(2,1)S(1)}, u32[]{:S(2)}, u32[]{:S(2)}) %collective-permute-start.40) | collective-permute-done | bytes 524320 | tf_op jit(solution)/shard_map/ppermute | solution.py:347
  119.7 7.1 %collective-permute-done.41 = bf16[256,512]{1,0:T(8,128)(2,1)S(1)} collective-permute-done((bf16[256,512]{1,0:T(8,128)(2,1)S(1)}, bf16[256,512]{1,0:T(8,128)(2,1)S(1)}, u32[]{:S(2)}, u32[]{:S(2)}) %collective-permute-start.41) | collective-permute-done | bytes 262176 | tf_op jit(solution)/shard_map/ppermute | solution.py:347
  129.6 2.4 %collective-permute-done.42 = bf16[128,512]{1,0:T(8,128)(2,1)S(1)} collective-permute-done((bf16[128,512]{1,0:T(8,128)(2,1)S(1)}, bf16[128,512]{1,0:T(8,128)(2,1)S(1)}, u32[]{:S(2)}, u32[]{:S(2)}) %collective-permute-start.42) | collective-permute-done | bytes 131104 | tf_op jit(solution)/shard_map/ppermute | solution.py:347
  132.0 2.5 %collective-permute-start.43 = (bf16[64,512]{1,0:T(8,128)(2,1)S(1)}, bf16[64,512]{1,0:T(8,128)(2,1)S(1)}, u32[]{:S(2)}, u32[]{:S(2)}) collective-permute-start(bf16[64,512]{1,0:T(8,128)(2,1)S(1)} %constant_dynamic-slice_fusion), channel_id=1, source_target_pairs={{0,2},{1,3},{2,0},{3,1},{4,6},{5,7},{6,4},{7,5},{8,10},{9,11},{10,... | collective-permute-start | bytes 196616 | tf_op jit(solution)/shard_map/ppermute | solution.py:347
  134.5 2.6 %collective-permute-done.30 = bf16[128,2560]{1,0:T(8,128)(2,1)S(1)} collective-permute-done((bf16[128,2560]{1,0:T(8,128)(2,1)S(1)}, bf16[128,2560]{1,0:T(8,128)(2,1)S(1)}, u32[]{:S(2)}, u32[]{:S(2)}) %collective-permute-start.30) | collective-permute-done | bytes 655392 | tf_op jit(solution)/shard_map/ppermute | solution.py:347
  137.3 2.5 %collective-permute-start.44 = (bf16[64,512]{1,0:T(8,128)(2,1)S(1)}, bf16[64,512]{1,0:T(8,128)(2,1)S(1)}, u32[]{:S(2)}, u32[]{:S(2)}) collective-permute-start(bf16[64,512]{1,0:T(8,128)(2,1)S(1)} %add_convert_fusion.15), channel_id=1, source_target_pairs={{0,2},{1,3},{2,0},{3,1},{4,6},{5,7},{6,4},{7,5},{8,10},{9,11},{10,... | collective-permute-start | bytes 196616 | tf_op jit(solution)/shard_map/ppermute | solution.py:347
  142.7 3.6 %collective-permute-start.45 = (bf16[128,512]{1,0:T(8,128)(2,1)S(1)}, bf16[128,512]{1,0:T(8,128)(2,1)S(1)}, u32[]{:S(2)}, u32[]{:S(2)}) collective-permute-start(bf16[128,512]{1,0:T(8,128)(2,1)S(1)} %maximum_select_fusion.13), channel_id=1, source_target_pairs={{0,1},{1,0},{2,3},{3,2},{4,5},{5,4},{6,7},{7,6},{8,9},{9,8},{10,11... | collective-permute-start | bytes 393224 | tf_op jit(solution)/shard_map/ppermute | solution.py:347
  147.3 3.2 %collective-permute-done.45 = bf16[128,512]{1,0:T(8,128)(2,1)S(1)} collective-permute-done((bf16[128,512]{1,0:T(8,128)(2,1)S(1)}, bf16[128,512]{1,0:T(8,128)(2,1)S(1)}, u32[]{:S(2)}, u32[]{:S(2)}) %collective-permute-start.45) | collective-permute-done | bytes 131104 | tf_op jit(solution)/shard_map/ppermute | solution.py:347
  154.0 3.5 %collective-permute-done.32 = bf16[32,2560]{1,0:T(8,128)(2,1)S(1)} collective-permute-done((bf16[32,2560]{1,0:T(8,128)(2,1)S(1)}, bf16[32,2560]{1,0:T(8,128)(2,1)S(1)}, u32[]{:S(2)}, u32[]{:S(2)}) %collective-permute-start.32) | collective-permute-done | bytes 163872 | tf_op jit(solution)/shard_map/ppermute | solution.py:347
  157.5 2.5 %collective-permute-start.33 = (bf16[16,2560]{1,0:T(8,128)(2,1)S(1)}, bf16[16,2560]{1,0:T(8,128)(2,1)S(1)}, u32[]{:S(2)}, u32[]{:S(2)}) collective-permute-start(bf16[16,2560]{1,0:T(8,128)(2,1)S(1)} %constant_dynamic-slice_fusion.5), channel_id=1, source_target_pairs={{0,2},{1,3},{2,0},{3,1},{4,6},{5,7},{6,4},{7,5},{8,10},{9,11},{10,... | collective-permute-start | bytes 245768 | tf_op jit(solution)/shard_map/ppermute | solution.py:347
  160.0 2.9 %collective-permute-done.33 = bf16[16,2560]{1,0:T(8,128)(2,1)S(1)} collective-permute-done((bf16[16,2560]{1,0:T(8,128)(2,1)S(1)}, bf16[16,2560]{1,0:T(8,128)(2,1)S(1)}, u32[]{:S(2)}, u32[]{:S(2)}) %collective-permute-start.33) | collective-permute-done | bytes 81952 | tf_op jit(solution)/shard_map/ppermute | solution.py:347
  162.9 3.3 %collective-permute-start.34 = (bf16[16,2560]{1,0:T(8,128)(2,1)S(1)}, bf16[16,2560]{1,0:T(8,128)(2,1)S(1)}, u32[]{:S(2)}, u32[]{:S(2)}) collective-permute-start(bf16[16,2560]{1,0:T(8,128)(2,1)S(1)} %add_convert_fusion.14), channel_id=1, source_target_pairs={{0,2},{1,3},{2,0},{3,1},{4,6},{5,7},{6,4},{7,5},{8,10},{9,11},{10,... | collective-permute-start | bytes 245768 | tf_op jit(solution)/shard_map/ppermute | solution.py:347
  166.4 2.3 %collective-permute-done.34 = bf16[16,2560]{1,0:T(8,128)(2,1)S(1)} collective-permute-done((bf16[16,2560]{1,0:T(8,128)(2,1)S(1)}, bf16[16,2560]{1,0:T(8,128)(2,1)S(1)}, u32[]{:S(2)}, u32[]{:S(2)}) %collective-permute-start.34) | collective-permute-done | bytes 81952 | tf_op jit(solution)/shard_map/ppermute | solution.py:347
  168.7 2.3 %collective-permute-start.35 = (bf16[32,2560]{1,0:T(8,128)(2,1)S(1)}, bf16[32,2560]{1,0:T(8,128)(2,1)S(1)}, u32[]{:S(2)}, u32[]{:S(2)}) collective-permute-start(bf16[32,2560]{1,0:T(8,128)(2,1)S(1)} %maximum_select_fusion.12), channel_id=1, source_target_pairs={{0,1},{1,0},{2,3},{3,2},{4,5},{5,4},{6,7},{7,6},{8,9},{9,8},{10,11... | collective-permute-start | bytes 491528 | tf_op jit(solution)/shard_map/ppermute | solution.py:347
  171.4 3.2 %collective-permute-start.24 = (bf16[16,1536]{1,0:T(8,128)(2,1)S(1)}, bf16[16,1536]{1,0:T(8,128)(2,1)S(1)}, u32[]{:S(2)}, u32[]{:S(2)}) collective-permute-start(bf16[16,1536]{1,0:T(8,128)(2,1)S(1)} %add_convert_fusion.16), channel_id=1, source_target_pairs={{0,2},{1,3},{2,0},{3,1},{4,6},{5,7},{6,4},{7,5},{8,10},{9,11},{10,... | collective-permute-start | bytes 147464 | tf_op jit(solution)/shard_map/ppermute | solution.py:347
  174.7 3.0 %collective-permute-start.36 = (bf16[64,2560]{1,0:T(8,128)(2,1)S(1)}, bf16[64,2560]{1,0:T(8,128)(2,1)S(1)}, u32[]{:S(2)}, u32[]{:S(2)}) collective-permute-start(bf16[64,2560]{1,0:T(8,128)(2,1)S(1)} %maximum_select_fusion.9), channel_id=1, source_target_pairs={{0,8},{4,12},{8,0},{12,4},{16,24},{20,28},{24,16},{28,20},{1,9},{5... | collective-permute-start | bytes 983048 | tf_op jit(solution)/shard_map/ppermute | solution.py:347
  178.8 3.9 %collective-permute-done.36 = bf16[64,2560]{1,0:T(8,128)(2,1)S(1)} collective-permute-done((bf16[64,2560]{1,0:T(8,128)(2,1)S(1)}, bf16[64,2560]{1,0:T(8,128)(2,1)S(1)}, u32[]{:S(2)}, u32[]{:S(2)}) %collective-permute-start.36) | collective-permute-done | bytes 327712 | tf_op jit(solution)/shard_map/ppermute | solution.py:347
  185.7 9.9 %collective-permute-done.26 = bf16[64,1536]{1,0:T(8,128)(2,1)S(1)} collective-permute-done((bf16[64,1536]{1,0:T(8,128)(2,1)S(1)}, bf16[64,1536]{1,0:T(8,128)(2,1)S(1)}, u32[]{:S(2)}, u32[]{:S(2)}) %collective-permute-start.26) | collective-permute-done | bytes 196640 | tf_op jit(solution)/shard_map/ppermute | solution.py:347
  198.9 6.7 %collective-permute-done.27 = bf16[128,1536]{1,0:T(8,128)(2,1)S(1)} collective-permute-done((bf16[128,1536]{1,0:T(8,128)(2,1)S(1)}, bf16[128,1536]{1,0:T(8,128)(2,1)S(1)}, u32[]{:S(2)}, u32[]{:S(2)}) %collective-permute-start.27) | collective-permute-done | bytes 393248 | tf_op jit(solution)/shard_map/ppermute | solution.py:347
  208.2 2.6 %fusion.1 = f32[2048,512]{1,0:T(8,128)} fusion(bf16[1024,512]{1,0:T(8,128)(2,1)S(1)} %collective-permute-done.48, bf16[1024,512]{1,0:T(8,128)(2,1)S(1)} %maximum_select_fusion.4, pred[]{:T(512)S(6)} %eq.50), kind=kLoop, calls=%fused_computation.10 | loop fusion | flops 10485760 | bytes 6291457 | tf_op jit(solution)/shard_map/convert_element_type | solution.py:487
  210.8 2.3 %fusion.2 = f32[512,1536]{1,0:T(8,128)} fusion(bf16[256,1536]{1,0:T(8,128)(2,1)S(1)} %collective-permute-done.28, bf16[256,1536]{1,0:T(8,128)(2,1)S(1)} %maximum_select_fusion.5, pred[]{:T(512)S(6)} %eq.50), kind=kLoop, calls=%fused_computation.14 | loop fusion | flops 7864320 | bytes 4718593 | tf_op jit(solution)/shard_map/convert_element_type | solution.py:487
  214.9 2.4 %slice.147 = f32[512,2048]{1,0:T(8,128)} slice(f32[512,2560]{1,0:T(8,128)S(1)} %fusion), slice={[0:512], [0:2048]} | slice | bytes 8388608 | tf_op jit(solution)/shard_map/slice | solution.py:517
  (235 shorter events, 69.4 us)
Async XLA Ops:
  2.0 10.0 %collective-permute-start = (bf16[128,512]{1,0:T(8,128)(2,1)S(1)}, bf16[128,512]{1,0:T(8,128)(2,1)S(1)}, u32[]{:S(2)}, u32[]{:S(2)}) collective-permute-start(bf16[128,512]{1,0:T(8,128)(2,1)S(1)} %get-tuple-element.99), channel_id=1, source_target_pairs={{0,8},{4,12},{8,0},{12,4},{16,24},{20,28},{24,16},{28,20},{1,9},{5... | collective-permute-start | bytes 393224 | tf_op jit(solution)/shard_map/ppermute | solution.py:400
  5.0 7.4 %collective-permute-start.1 = (bf16[128,512]{1,0:T(8,128)(2,1)S(1)}, bf16[128,512]{1,0:T(8,128)(2,1)S(1)}, u32[]{:S(2)}, u32[]{:S(2)}) collective-permute-start(bf16[128,512]{1,0:T(8,128)(2,1)S(1)} %get-tuple-element.101), channel_id=1, source_target_pairs={{0,16},{4,20},{8,24},{12,28},{16,0},{20,4},{24,8},{28,12},{1,17},{... | collective-permute-start | bytes 393224 | tf_op jit(solution)/shard_map/ppermute | solution.py:400
  6.5 7.1 %collective-permute-start.2 = (bf16[128,512]{1,0:T(8,128)(2,1)S(1)}, bf16[128,512]{1,0:T(8,128)(2,1)S(1)}, u32[]{:S(2)}, u32[]{:S(2)}) collective-permute-start(bf16[128,512]{1,0:T(8,128)(2,1)S(1)} %get-tuple-element.98), channel_id=1, source_target_pairs={{0,24},{4,28},{8,16},{12,20},{16,8},{20,12},{24,0},{28,4},{1,25},{... | collective-permute-start | bytes 393224 | tf_op jit(solution)/shard_map/ppermute | solution.py:400
  8.4 24.3 %collective-permute-start.3 = (bf16[128,512]{1,0:T(8,128)(2,1)}, bf16[128,512]{1,0:T(8,128)(2,1)S(1)}, u32[]{:S(2)}, u32[]{:S(2)}) collective-permute-start(bf16[128,512]{1,0:T(8,128)(2,1)} %get-tuple-element.95), channel_id=1, source_target_pairs={{0,8},{4,12},{8,0},{12,4},{16,24},{20,28},{24,16},{28,20},{1,9},{5... | collective-permute-start | bytes 393224 | tf_op jit(solution)/shard_map/ppermute | solution.py:400
  10.3 22.4 %collective-permute-start.4 = (bf16[128,512]{1,0:T(8,128)(2,1)}, bf16[128,512]{1,0:T(8,128)(2,1)S(1)}, u32[]{:S(2)}, u32[]{:S(2)}) collective-permute-start(bf16[128,512]{1,0:T(8,128)(2,1)} %get-tuple-element.97), channel_id=1, source_target_pairs={{0,16},{4,20},{8,24},{12,28},{16,0},{20,4},{24,8},{28,12},{1,17},{... | collective-permute-start | bytes 393224 | tf_op jit(solution)/shard_map/ppermute | solution.py:400
  12.0 20.7 %collective-permute-start.5 = (bf16[128,512]{1,0:T(8,128)(2,1)}, bf16[128,512]{1,0:T(8,128)(2,1)S(1)}, u32[]{:S(2)}, u32[]{:S(2)}) collective-permute-start(bf16[128,512]{1,0:T(8,128)(2,1)} %get-tuple-element.94), channel_id=1, source_target_pairs={{0,24},{4,28},{8,16},{12,20},{16,8},{20,12},{24,0},{28,4},{1,25},{... | collective-permute-start | bytes 393224 | tf_op jit(solution)/shard_map/ppermute | solution.py:400
  64.4 16.1 %collective-permute-start.10 = (bf16[512,1024]{1,0:T(8,128)(2,1)}, bf16[512,1024]{1,0:T(8,128)(2,1)}, u32[]{:S(2)}, u32[]{:S(2)}) collective-permute-start(bf16[512,1024]{1,0:T(8,128)(2,1)} %pad_maximum_fusion.1), channel_id=1, source_target_pairs={{0,4},{4,0},{8,12},{12,8},{16,20},{20,16},{24,28},{28,24},{1,5},{5... | collective-permute-start | bytes 3145736 | tf_op jit(solution)/shard_map/ppermute | solution.py:347
  65.4 13.2 %collective-permute-start.9 = (bf16[128,512]{1,0:T(8,128)(2,1)}, bf16[128,512]{1,0:T(8,128)(2,1)}, u32[]{:S(2)}, u32[]{:S(2)}) collective-permute-start(bf16[128,512]{1,0:T(8,128)(2,1)} %get-tuple-element.91), channel_id=1, source_target_pairs={{0,24},{4,28},{8,16},{12,20},{16,8},{20,12},{24,0},{28,4},{1,25},{... | collective-permute-start | bytes 393224 | tf_op jit(solution)/shard_map/ppermute | solution.py:400
  66.8 12.4 %collective-permute-start.8 = (bf16[128,512]{1,0:T(8,128)(2,1)}, bf16[128,512]{1,0:T(8,128)(2,1)}, u32[]{:S(2)}, u32[]{:S(2)}) collective-permute-start(bf16[128,512]{1,0:T(8,128)(2,1)} %get-tuple-element.92), channel_id=1, source_target_pairs={{0,16},{4,20},{8,24},{12,28},{16,0},{20,4},{24,8},{28,12},{1,17},{... | collective-permute-start | bytes 393224 | tf_op jit(solution)/shard_map/ppermute | solution.py:400
  68.1 11.1 %collective-permute-start.7 = (bf16[128,512]{1,0:T(8,128)(2,1)}, bf16[128,512]{1,0:T(8,128)(2,1)}, u32[]{:S(2)}, u32[]{:S(2)}) collective-permute-start(bf16[128,512]{1,0:T(8,128)(2,1)} %get-tuple-element.93), channel_id=1, source_target_pairs={{0,8},{4,12},{8,0},{12,4},{16,24},{20,28},{24,16},{28,20},{1,9},{5... | collective-permute-start | bytes 393224 | tf_op jit(solution)/shard_map/ppermute | solution.py:400
  74.0 32.6 %collective-permute-start.29 = (bf16[256,2560]{1,0:T(8,128)(2,1)}, bf16[256,2560]{1,0:T(8,128)(2,1)S(1)}, u32[]{:S(2)}, u32[]{:S(2)}) collective-permute-start(bf16[256,2560]{1,0:T(8,128)(2,1)} %fusion.3), channel_id=1, source_target_pairs={{0,4},{4,0},{8,12},{12,8},{16,20},{20,16},{24,28},{28,24},{1,5},{5... | collective-permute-start | bytes 3932168 | tf_op jit(solution)/shard_map/ppermute | solution.py:347
  78.6 17.9 %collective-permute-start.39 = (bf16[1024,512]{1,0:T(8,128)(2,1)S(1)}, bf16[1024,512]{1,0:T(8,128)(2,1)S(1)}, u32[]{:S(2)}, u32[]{:S(2)}) collective-permute-start(bf16[1024,512]{1,0:T(8,128)(2,1)S(1)} %constant_dynamic-slice_fusion.4), channel_id=1, source_target_pairs={{0,4},{4,0},{8,12},{12,8},{16,20},{20,16},{24,28},{28,24},{1,5},{5... | collective-permute-start | bytes 3145736 | tf_op jit(solution)/shard_map/ppermute | solution.py:347
  85.6 120.2 %collective-permute-start.13 = (bf16[128,512]{1,0:T(8,128)(2,1)S(1)}, bf16[128,512]{1,0:T(8,128)(2,1)S(1)}, u32[]{:S(2)}, u32[]{:S(2)}) collective-permute-start(bf16[128,512]{1,0:T(8,128)(2,1)S(1)} %get-tuple-element.83), channel_id=1, source_target_pairs={{0,24},{4,28},{8,16},{12,20},{16,8},{20,12},{24,0},{28,4},{1,25},{... | collective-permute-start | bytes 393224 | tf_op jit(solution)/shard_map/ppermute | solution.py:400
  87.1 119.2 %collective-permute-start.12 = (bf16[128,512]{1,0:T(8,128)(2,1)S(1)}, bf16[128,512]{1,0:T(8,128)(2,1)S(1)}, u32[]{:S(2)}, u32[]{:S(2)}) collective-permute-start(bf16[128,512]{1,0:T(8,128)(2,1)S(1)} %get-tuple-element.84), channel_id=1, source_target_pairs={{0,16},{4,20},{8,24},{12,28},{16,0},{20,4},{24,8},{28,12},{1,17},{... | collective-permute-start | bytes 393224 | tf_op jit(solution)/shard_map/ppermute | solution.py:400
  96.5 31.9 %collective-permute-start.19 = (bf16[256,1536]{1,0:T(8,128)(2,1)S(1)}, bf16[256,1536]{1,0:T(8,128)(2,1)S(1)}, u32[]{:S(2)}, u32[]{:S(2)}) collective-permute-start(bf16[256,1536]{1,0:T(8,128)(2,1)S(1)} %constant_dynamic-slice_fusion.13), channel_id=1, source_target_pairs={{0,4},{4,0},{8,12},{12,8},{16,20},{20,16},{24,28},{28,24},{1,5},{5... | collective-permute-start | bytes 2359304 | tf_op jit(solution)/shard_map/ppermute | solution.py:347
  105.3 12.0 %collective-permute-start.40 = (bf16[512,512]{1,0:T(8,128)(2,1)S(1)}, bf16[512,512]{1,0:T(8,128)(2,1)S(1)}, u32[]{:S(2)}, u32[]{:S(2)}) collective-permute-start(bf16[512,512]{1,0:T(8,128)(2,1)S(1)} %constant_dynamic-slice_fusion.3), channel_id=1, source_target_pairs={{0,8},{4,12},{8,0},{12,4},{16,24},{20,28},{24,16},{28,20},{1,9},{5... | collective-permute-start | bytes 1572872 | tf_op jit(solution)/shard_map/ppermute | solution.py:347
  117.5 9.3 %collective-permute-start.41 = (bf16[256,512]{1,0:T(8,128)(2,1)S(1)}, bf16[256,512]{1,0:T(8,128)(2,1)S(1)}, u32[]{:S(2)}, u32[]{:S(2)}) collective-permute-start(bf16[256,512]{1,0:T(8,128)(2,1)S(1)} %constant_dynamic-slice_fusion.2), channel_id=1, source_target_pairs={{0,16},{4,20},{8,24},{12,28},{16,0},{20,4},{24,8},{28,12},{1,17},{... | collective-permute-start | bytes 786440 | tf_op jit(solution)/shard_map/ppermute | solution.py:347
  118.3 18.8 %collective-permute-start.30 = (bf16[128,2560]{1,0:T(8,128)(2,1)S(1)}, bf16[128,2560]{1,0:T(8,128)(2,1)S(1)}, u32[]{:S(2)}, u32[]{:S(2)}) collective-permute-start(bf16[128,2560]{1,0:T(8,128)(2,1)S(1)} %constant_dynamic-slice_fusion.8), channel_id=1, source_target_pairs={{0,16},{4,20},{8,24},{12,28},{16,0},{20,4},{24,8},{28,12},{1,17},{... | collective-permute-start | bytes 1966088 | tf_op jit(solution)/shard_map/ppermute | solution.py:347
  128.7 17.6 %collective-permute-start.20 = (bf16[128,1536]{1,0:T(8,128)(2,1)S(1)}, bf16[128,1536]{1,0:T(8,128)(2,1)S(1)}, u32[]{:S(2)}, u32[]{:S(2)}) collective-permute-start(bf16[128,1536]{1,0:T(8,128)(2,1)S(1)} %constant_dynamic-slice_fusion.12), channel_id=1, source_target_pairs={{0,8},{4,12},{8,0},{12,4},{16,24},{20,28},{24,16},{28,20},{1,9},{5... | collective-permute-start | bytes 1179656 | tf_op jit(solution)/shard_map/ppermute | solution.py:347
  139.9 11.7 %collective-permute-start.31 = (bf16[64,2560]{1,0:T(8,128)(2,1)S(1)}, bf16[64,2560]{1,0:T(8,128)(2,1)S(1)}, u32[]{:S(2)}, u32[]{:S(2)}) collective-permute-start(bf16[64,2560]{1,0:T(8,128)(2,1)S(1)} %constant_dynamic-slice_fusion.7), channel_id=1, source_target_pairs={{0,8},{4,12},{8,0},{12,4},{16,24},{20,28},{24,16},{28,20},{1,9},{5... | collective-permute-start | bytes 983048 | tf_op jit(solution)/shard_map/ppermute | solution.py:347
  142.7 7.9 %collective-permute-start.45 = (bf16[128,512]{1,0:T(8,128)(2,1)S(1)}, bf16[128,512]{1,0:T(8,128)(2,1)S(1)}, u32[]{:S(2)}, u32[]{:S(2)}) collective-permute-start(bf16[128,512]{1,0:T(8,128)(2,1)S(1)} %maximum_select_fusion.13), channel_id=1, source_target_pairs={{0,1},{1,0},{2,3},{3,2},{4,5},{5,4},{6,7},{7,6},{8,9},{9,8},{10,11... | collective-permute-start | bytes 393224 | tf_op jit(solution)/shard_map/ppermute | solution.py:347
  146.4 7.4 %collective-permute-start.21 = (bf16[64,1536]{1,0:T(8,128)(2,1)S(1)}, bf16[64,1536]{1,0:T(8,128)(2,1)S(1)}, u32[]{:S(2)}, u32[]{:S(2)}) collective-permute-start(bf16[64,1536]{1,0:T(8,128)(2,1)S(1)} %constant_dynamic-slice_fusion.11), channel_id=1, source_target_pairs={{0,16},{4,20},{8,24},{12,28},{16,0},{20,4},{24,8},{28,12},{1,17},{... | collective-permute-start | bytes 589832 | tf_op jit(solution)/shard_map/ppermute | solution.py:347
  150.6 27.1 %collective-permute-start.46 = (bf16[256,512]{1,0:T(8,128)(2,1)S(1)}, bf16[256,512]{1,0:T(8,128)(2,1)S(1)}, u32[]{:S(2)}, u32[]{:S(2)}) collective-permute-start(bf16[256,512]{1,0:T(8,128)(2,1)S(1)} %maximum_select_fusion.10), channel_id=1, source_target_pairs={{0,16},{4,20},{8,24},{12,28},{16,0},{20,4},{24,8},{28,12},{1,17},{... | collective-permute-start | bytes 786440 | tf_op jit(solution)/shard_map/ppermute | solution.py:347
  171.4 6.6 %collective-permute-start.24 = (bf16[16,1536]{1,0:T(8,128)(2,1)S(1)}, bf16[16,1536]{1,0:T(8,128)(2,1)S(1)}, u32[]{:S(2)}, u32[]{:S(2)}) collective-permute-start(bf16[16,1536]{1,0:T(8,128)(2,1)S(1)} %add_convert_fusion.16), channel_id=1, source_target_pairs={{0,2},{1,3},{2,0},{3,1},{4,6},{5,7},{6,4},{7,5},{8,10},{9,11},{10,... | collective-permute-start | bytes 147464 | tf_op jit(solution)/shard_map/ppermute | solution.py:347
  174.7 8.1 %collective-permute-start.36 = (bf16[64,2560]{1,0:T(8,128)(2,1)S(1)}, bf16[64,2560]{1,0:T(8,128)(2,1)S(1)}, u32[]{:S(2)}, u32[]{:S(2)}) collective-permute-start(bf16[64,2560]{1,0:T(8,128)(2,1)S(1)} %maximum_select_fusion.9), channel_id=1, source_target_pairs={{0,8},{4,12},{8,0},{12,4},{16,24},{20,28},{24,16},{28,20},{1,9},{5... | collective-permute-start | bytes 983048 | tf_op jit(solution)/shard_map/ppermute | solution.py:347
  177.9 19.8 %collective-permute-start.47 = (bf16[512,512]{1,0:T(8,128)(2,1)S(1)}, bf16[512,512]{1,0:T(8,128)(2,1)S(1)}, u32[]{:S(2)}, u32[]{:S(2)}) collective-permute-start(bf16[512,512]{1,0:T(8,128)(2,1)S(1)} %maximum_select_fusion.7), channel_id=1, source_target_pairs={{0,8},{4,12},{8,0},{12,4},{16,24},{20,28},{24,16},{28,20},{1,9},{5... | collective-permute-start | bytes 1572872 | tf_op jit(solution)/shard_map/ppermute | solution.py:347
  182.9 15.7 %collective-permute-start.37 = (bf16[128,2560]{1,0:T(8,128)(2,1)S(1)}, bf16[128,2560]{1,0:T(8,128)(2,1)S(1)}, u32[]{:S(2)}, u32[]{:S(2)}) collective-permute-start(bf16[128,2560]{1,0:T(8,128)(2,1)S(1)} %maximum_select_fusion.6), channel_id=1, source_target_pairs={{0,16},{4,20},{8,24},{12,28},{16,0},{20,4},{24,8},{28,12},{1,17},{... | collective-permute-start | bytes 1966088 | tf_op jit(solution)/shard_map/ppermute | solution.py:347
  183.0 12.6 %collective-permute-start.26 = (bf16[64,1536]{1,0:T(8,128)(2,1)S(1)}, bf16[64,1536]{1,0:T(8,128)(2,1)S(1)}, u32[]{:S(2)}, u32[]{:S(2)}) collective-permute-start(bf16[64,1536]{1,0:T(8,128)(2,1)S(1)} %maximum_select_fusion.11), channel_id=1, source_target_pairs={{0,16},{4,20},{8,24},{12,28},{16,0},{20,4},{24,8},{28,12},{1,17},{... | collective-permute-start | bytes 589832 | tf_op jit(solution)/shard_map/ppermute | solution.py:347
  195.6 10.7 %collective-permute-start.11 = (bf16[128,512]{1,0:T(8,128)(2,1)S(1)}, bf16[128,512]{1,0:T(8,128)(2,1)S(1)}, u32[]{:S(2)}, u32[]{:S(2)}) collective-permute-start(bf16[128,512]{1,0:T(8,128)(2,1)S(1)} %get-tuple-element.85), channel_id=1, source_target_pairs={{0,8},{4,12},{8,0},{12,4},{16,24},{20,28},{24,16},{28,20},{1,9},{5... | collective-permute-start | bytes 393224 | tf_op jit(solution)/shard_map/ppermute | solution.py:400
  197.7 7.8 %collective-permute-start.27 = (bf16[128,1536]{1,0:T(8,128)(2,1)S(1)}, bf16[128,1536]{1,0:T(8,128)(2,1)S(1)}, u32[]{:S(2)}, u32[]{:S(2)}) collective-permute-start(bf16[128,1536]{1,0:T(8,128)(2,1)S(1)} %maximum_select_fusion.8), channel_id=1, source_target_pairs={{0,8},{4,12},{8,0},{12,4},{16,24},{20,28},{24,16},{28,20},{1,9},{5... | collective-permute-start | bytes 1179656 | tf_op jit(solution)/shard_map/ppermute | solution.py:347
  198.5 9.7 %collective-permute-start.48 = (bf16[1024,512]{1,0:T(8,128)(2,1)S(1)}, bf16[1024,512]{1,0:T(8,128)(2,1)S(1)}, u32[]{:S(2)}, u32[]{:S(2)}) collective-permute-start(bf16[1024,512]{1,0:T(8,128)(2,1)S(1)} %maximum_select_fusion.4), channel_id=1, source_target_pairs={{0,4},{4,0},{8,12},{12,8},{16,20},{20,16},{24,28},{28,24},{1,5},{5... | collective-permute-start | bytes 3145736 | tf_op jit(solution)/shard_map/ppermute | solution.py:347
  205.6 7.6 %collective-permute-start.38 = (bf16[256,2560]{1,0:T(8,128)(2,1)S(1)}, bf16[256,2560]{1,0:T(8,128)(2,1)S(1)}, u32[]{:S(2)}, u32[]{:S(2)}) collective-permute-start(bf16[256,2560]{1,0:T(8,128)(2,1)S(1)} %maximum_select_fusion.3), channel_id=1, source_target_pairs={{0,4},{4,0},{8,12},{12,8},{16,20},{20,16},{24,28},{28,24},{1,5},{5... | collective-permute-start | bytes 3932168 | tf_op jit(solution)/shard_map/ppermute | solution.py:347
  (52 other events, 370.6 us)
